TPU v7x, 512 devices: a whole 4x8x8 slice. The times are simulated.
512 devices in a mesh: grp: 32 (over y, x_hi, core), frq: 16 (over z, x_lo).
Axes of the slice: x: 4 (x_hi: 2, x_lo: 2; x = x_hi * 2 + x_lo), y: 8, z: 8, core: 2. Of those that a mesh axis runs over, the one named last changes fastest.
Arguments:
- spectra: bfloat16 [32, 512, 240, 128], P('grp', 'frq'), may hold values from -6 to 6
- band_weight: float32 [512], replicated, may hold values from 0.25 to 4
Outputs:
- correlations: bfloat16 [2, 32, 4096, 1024], P(None, 'grp', 'frq')
All inputs are finite; a program needn't handle non-finite values.
Results may differ from a plain program's by a relative error of at most 0.0058.
Values may be sent and summed in bfloat16 or wider, within the bound.
A program may use at most 64 MiB of HBM per device.

v0:
```python
import math

import jax
import jax.numpy as jnp
from jax import lax
from jax.sharding import PartitionSpec as P

ROUNDS = 2


def passed_along(value, axis, steps):
    count = lax.axis_size(axis)
    pairs = [(source, (source + steps) % count) for source in range(count)]
    return lax.ppermute(value, axis, pairs)


def inverse_table(band_weight):
    bin_count = band_weight.shape[0]
    lag_count = 2 * bin_count
    phase_index = (
        jnp.arange(bin_count, dtype=jnp.int32)[:, None]
        * jnp.arange(lag_count, dtype=jnp.int32)[None, :]
        % lag_count
    )
    phase_angle = phase_index.astype(jnp.float32) * (2.0 * math.pi / lag_count)
    weighting = band_weight[:, None] * (1.0 / math.sqrt(bin_count))
    return jnp.stack(
        [weighting * jnp.cos(phase_angle), -weighting * jnp.sin(phase_angle)], 1
    ).astype(jnp.bfloat16)


def cross_stack(local_block, partner_block):
    windows = local_block.shape[1]
    half_width = local_block.shape[2] // 2
    product = jnp.einsum(
        "fwa,fwb->fab", local_block, partner_block, preferred_element_type=jnp.float32
    )
    real_part = product[:, :half_width, :half_width] + product[:, half_width:, half_width:]
    imag_part = product[:, half_width:, :half_width] - product[:, :half_width, half_width:]
    scaled = jnp.stack([real_part, imag_part], 1) * (1.0 / math.sqrt(windows))
    return scaled.reshape(scaled.shape[0], 2, half_width * half_width).astype(jnp.bfloat16)


def local(spectra, band_weight):
    lag_table = inverse_table(band_weight)
    local_block = spectra[0]
    partner_block = spectra
    cross_list = []
    for turn_index in range(ROUNDS):
        partner_block = passed_along(spectra, "grp", turn_index + 1)
        cross_list.append(cross_stack(local_block, partner_block[0]))

    def to_lags(gathered):
        lagged = jnp.einsum(
            "nfcp,fcl->npl", gathered, lag_table, preferred_element_type=jnp.float32
        )
        return lagged.astype(jnp.bfloat16)

    result = jnp.concatenate(
        [
            to_lags(lax.all_to_all(member[None], "frq", split_axis=3, concat_axis=1, tiled=True))
            for member in cross_list
        ],
        0,
    )
    return result[:, None]


def solution(mesh):
    return jax.shard_map(
        local,
        mesh=mesh,
        in_specs=(P("grp", "frq", None, None), P()),
        out_specs=P(None, "grp", "frq", None),
        check_vma=False,
    )
```

profile of v0, /device:TPU:2, one launch (start us, length us, event | category | flops | bytes accessed | tf_op | source)
XLA Modules:
  0.0 122.3 jit_solution(1366987592506113461)
XLA Ops:
  0.0 4.0 %collective-permute-start.1 = (bf16[1,32,240,128]{3,2,1,0:T(8,128)(2,1)}, bf16[1,32,240,128]{3,2,1,0:T(8,128)(2,1)S(1)}, u32[]{:S(2)}, u32[]{:S(2)}) collective-permute-start(bf16[1,32,240,128]{3,2,1,0:T(8,128)(2,1)} %param.2), channel_id=1, source_target_pairs={{0,32},{16,48},{32,64},{48,80},{64,96},{80,112},{96,128},{112,144}... | collective-permute-start | bytes 5898248 | tf_op jit(solution)/shard_map/ppermute | solution.py:14
  4.0 1.9 %collective-permute-start = (bf16[1,32,240,128]{3,2,1,0:T(8,128)(2,1)}, bf16[1,32,240,128]{3,2,1,0:T(8,128)(2,1)}, u32[]{:S(2)}, u32[]{:S(2)}) collective-permute-start(bf16[1,32,240,128]{3,2,1,0:T(8,128)(2,1)} %param.2), channel_id=1, source_target_pairs={{0,16},{16,32},{32,48},{48,64},{64,80},{80,96},{96,112},{112,128},... | collective-permute-start | bytes 5898248 | tf_op jit(solution)/shard_map/ppermute | solution.py:14
  6.0 45.5 %collective-permute-done.1 = bf16[1,32,240,128]{3,2,1,0:T(8,128)(2,1)S(1)} collective-permute-done((bf16[1,32,240,128]{3,2,1,0:T(8,128)(2,1)}, bf16[1,32,240,128]{3,2,1,0:T(8,128)(2,1)S(1)}, u32[]{:S(2)}, u32[]{:S(2)}) %collective-permute-start.1) | collective-permute-done | bytes 1966112 | tf_op jit(solution)/shard_map/ppermute | solution.py:14
  51.4 2.4 %fusion.6 = f32[32,128,128]{2,1,0:T(8,128)S(1)} fusion(bf16[1,32,240,128]{3,2,1,0:T(8,128)(2,1)S(1)} %collective-permute-done.1, bf16[1,32,240,128]{3,2,1,0:T(8,128)(2,1)} %param.2), kind=kOutput, calls=%fused_computation.12 | convolution fusion | flops 251658240 | bytes 6029312 | tf_op jit(solution)/shard_map/fwa,fwb->fab/dot_general | solution.py:35
  53.8 0.6 slice_add_fusion
  54.4 0.4 stack.28
  54.8 0.4 stack.29
  55.1 0.1 fusion.17
  55.2 2.8 %copy.40 = bf16[1,32,2,4096]{1,2,0,3:T(2,128)(2,1)S(1)} copy(bf16[1,32,2,4096]{3,1,2,0:T(8,128)(2,1)S(1)} %fusion.17) | data formatting | bytes 1048576 | tf_op jit(solution)/shard_map/convert_element_type | solution.py:41
  58.0 2.7 %reshape.204 = bf16[16,2,8192]{2,1,0:T(2,128)(2,1)} reshape(bf16[4096,1,2,32]{3,2,1,0:T(2,128)(2,1)S(1)} %bitcast.47) | data formatting | bytes 1048576
  60.7 11.8 %all-to-all-start.1 = ((bf16[16,2,8192]{2,1,0:T(2,128)(2,1)}), bf16[16,2,8192]{2,1,0:T(2,128)(2,1)}, u32[]{:S(2)}, u32[]{:S(2)}) async-start(bf16[16,2,8192]{2,1,0:T(2,128)(2,1)} %reshape.204), calls=%async_computation.1 | async-start | bytes 1048576 | tf_op jit(solution)/shard_map/all_to_all | solution.py:61
  72.5 0.0 collective-permute-done
  72.5 3.0 %fusion.8 = f32[32,128,128]{2,1,0:T(8,128)S(1)} fusion(bf16[1,32,240,128]{3,2,1,0:T(8,128)(2,1)} %collective-permute-done, bf16[1,32,240,128]{3,2,1,0:T(8,128)(2,1)} %param.2), kind=kOutput, calls=%fused_computation.14 | convolution fusion | flops 251658240 | bytes 6029312 | tf_op jit(solution)/shard_map/fwa,fwb->fab/dot_general | solution.py:35
  75.4 0.6 slice_add_fusion.1
  76.1 0.4 stack.24
  76.4 0.4 stack.25
  76.8 0.1 fusion.16
  76.9 2.8 %copy.36 = bf16[1,32,2,4096]{1,2,0,3:T(2,128)(2,1)S(1)} copy(bf16[1,32,2,4096]{3,1,2,0:T(8,128)(2,1)S(1)} %fusion.16) | data formatting | bytes 1048576 | tf_op jit(solution)/shard_map/convert_element_type | solution.py:41
  79.6 0.0 copy-start.3
  79.7 2.6 %reshape.206 = bf16[16,2,8192]{2,1,0:T(2,128)(2,1)} reshape(bf16[4096,1,2,32]{3,2,1,0:T(2,128)(2,1)S(1)} %bitcast.48) | data formatting | bytes 1048576
  82.3 4.1 %all-to-all-done.1 = bf16[16,2,8192]{2,1,0:T(2,128)(2,1)} async-done(((bf16[16,2,8192]{2,1,0:T(2,128)(2,1)}), bf16[16,2,8192]{2,1,0:T(2,128)(2,1)}, u32[]{:S(2)}, u32[]{:S(2)}) %all-to-all-start.1) | async-done | bytes 524320 | tf_op jit(solution)/shard_map/all_to_all | solution.py:61
  86.4 9.5 %all-to-all-start = ((bf16[16,2,8192]{2,1,0:T(2,128)(2,1)}), bf16[16,2,8192]{2,1,0:T(2,128)(2,1)S(1)}, u32[]{:S(2)}, u32[]{:S(2)}) async-start(bf16[16,2,8192]{2,1,0:T(2,128)(2,1)} %reshape.206), calls=%async_computation | async-start | bytes 1048576 | tf_op jit(solution)/shard_map/all_to_all | solution.py:61
  95.9 0.0 copy-done.3
  95.9 9.6 %multiply_convert_fusion = (bf16[512,1,1024]{2,0,1:T(8,128)(2,1)}, bf16[512,1,1024]{2,0,1:T(8,128)(2,1)}) fusion(f32[512]{0:T(512)S(1)} %get-tuple-element.10, f32[512]{0:T(512)S(1)} %get-tuple-element.9), kind=kLoop, calls=%fused_computation.7 | loop fusion | flops 9437184 | bytes 2101248 | tf_op jit(solution)/shard_map/convert.1
  105.5 5.1 %reshape.205 = bf16[4096,1,2,32]{3,2,1,0:T(2,128)(2,1)S(1)} reshape(bf16[16,2,8192]{2,1,0:T(2,128)(2,1)} %all-to-all-done.1) | data formatting | bytes 1048576
  110.6 3.3 %copy.50 = bf16[1,32,2,16,256]{4,1,3,2,0:T(8,128)(2,1)} copy(bf16[1,32,2,16,256]{1,2,4,3,0:T(2,128)(2,1)S(1)} %bitcast.49) | data formatting | bytes 1048576 | tf_op jit(solution)/shard_map/all_to_all | solution.py:61
  113.9 0.0 all-to-all-done
  113.9 1.0 reshape.207
  115.0 0.0 copy-start
  115.0 3.3 %copy.48 = bf16[1,32,2,16,256]{4,1,3,2,0:T(8,128)(2,1)} copy(bf16[1,32,2,16,256]{1,2,4,3,0:T(2,128)(2,1)S(1)} %bitcast.50) | data formatting | bytes 1048576 | tf_op jit(solution)/shard_map/all_to_all | solution.py:61
  118.3 0.0 copy-done
  118.3 0.0 copy-start.1
  118.3 0.0 copy-start.2
  118.3 2.2 %fusion.14 = bf16[1,256,1024]{2,1,0:T(8,128)(2,1)S(1)} fusion(bf16[512,2,256]{2,0,1:T(8,128)(2,1)} %bitcast.51, bf16[512,1,1024]{2,0,1:T(8,128)(2,1)S(1)} %copy-done, bf16[512,1,1024]{2,0,1:T(8,128)(2,1)} %get-tuple-element.12), kind=kOutput, calls=%fused_computation.22 | convolution fusion | flops 538181632 | bytes 3145728 | tf_op jit(solution)/shard_map/nfcp,fcl->npl/dot_general | solution.py:54
  120.5 0.0 copy-done.1
  120.5 0.0 copy-done.2
  120.5 0.7 fusion.15
  121.3 1.1 maximum_bitcast_fusion
  (1 shorter events, 0.0 us)
Async XLA Ops:
  0.0 51.4 %collective-permute-start.1 = (bf16[1,32,240,128]{3,2,1,0:T(8,128)(2,1)}, bf16[1,32,240,128]{3,2,1,0:T(8,128)(2,1)S(1)}, u32[]{:S(2)}, u32[]{:S(2)}) collective-permute-start(bf16[1,32,240,128]{3,2,1,0:T(8,128)(2,1)} %param.2), channel_id=1, source_target_pairs={{0,32},{16,48},{32,64},{48,80},{64,96},{80,112},{96,128},{112,144}... | collective-permute-start | bytes 5898248 | tf_op jit(solution)/shard_map/ppermute | solution.py:14
  4.0 68.4 %collective-permute-start = (bf16[1,32,240,128]{3,2,1,0:T(8,128)(2,1)}, bf16[1,32,240,128]{3,2,1,0:T(8,128)(2,1)}, u32[]{:S(2)}, u32[]{:S(2)}) collective-permute-start(bf16[1,32,240,128]{3,2,1,0:T(8,128)(2,1)} %param.2), channel_id=1, source_target_pairs={{0,16},{16,32},{32,48},{48,64},{64,80},{80,96},{96,112},{112,128},... | collective-permute-start | bytes 5898248 | tf_op jit(solution)/shard_map/ppermute | solution.py:14
  60.7 25.8 %all-to-all-start.1 = ((bf16[16,2,8192]{2,1,0:T(2,128)(2,1)}), bf16[16,2,8192]{2,1,0:T(2,128)(2,1)}, u32[]{:S(2)}, u32[]{:S(2)}) async-start(bf16[16,2,8192]{2,1,0:T(2,128)(2,1)} %reshape.204), calls=%async_computation.1 | async-start | bytes 1048576 | tf_op jit(solution)/shard_map/all_to_all | solution.py:61
  79.6 16.2 %copy-start.3 = (f32[512]{0:T(512)S(1)}, f32[512]{0:T(512)}, u32[]{:S(2)}) copy-start(f32[512]{0:T(512)} %param.3) | copy-start | bytes 6148
  86.4 27.5 %all-to-all-start = ((bf16[16,2,8192]{2,1,0:T(2,128)(2,1)}), bf16[16,2,8192]{2,1,0:T(2,128)(2,1)S(1)}, u32[]{:S(2)}, u32[]{:S(2)}) async-start(bf16[16,2,8192]{2,1,0:T(2,128)(2,1)} %reshape.206), calls=%async_computation | async-start | bytes 1048576 | tf_op jit(solution)/shard_map/all_to_all | solution.py:61
  115.0 3.3 %copy-start = (bf16[512,1,1024]{2,0,1:T(8,128)(2,1)S(1)}, bf16[512,1,1024]{2,0,1:T(8,128)(2,1)}, u32[]{:S(2)}) copy-start(bf16[512,1,1024]{2,0,1:T(8,128)(2,1)} %get-tuple-element.11) | copy-start | bytes 3145732
  118.3 2.3 %copy-start.1 = (bf16[512,1,1024]{2,0,1:T(8,128)(2,1)S(1)}, bf16[512,1,1024]{2,0,1:T(8,128)(2,1)}, u32[]{:S(2)}) copy-start(bf16[512,1,1024]{2,0,1:T(8,128)(2,1)} %get-tuple-element.12) | copy-start | bytes 3145732
  118.3 2.3 %copy-start.2 = (bf16[1,32,2,16,256]{4,1,3,2,0:T(8,128)(2,1)S(1)}, bf16[1,32,2,16,256]{4,1,3,2,0:T(8,128)(2,1)}, u32[]{:S(2)}) copy-start(bf16[1,32,2,16,256]{4,1,3,2,0:T(8,128)(2,1)} %copy.48) | copy-start | bytes 1572868
where the time goes:
time: 123 us; the launch traced here: 122 us
  waiting for transfers between devices  49.6 us (40%)
  starting transfers between devices  27.2 us (22%)
  local copies, waits for them, and re-layouts  25 us (20%)
  other arithmetic  12.1 us (10%)
  matrix products  8.32 us (7%)
    ppermute x2, waiting for transfers between devices, passed_along(): return lax.ppermute(value, axis, pairs)  45.5 us
    all_to_all x2, starting transfers between devices, local(): lax.all_to_all(member[None], 'frq', split_axis=3, concat_axis=1, tiled=True)  21.3 us
    unnamed x12, local copies, waits for them, and re-layouts  11.4 us
    another operation x1, other arithmetic  9.6 us
    all_to_all x2, local copies, waits for them, and re-layouts, local(): lax.all_to_all(member[None], 'frq', split_axis=3, concat_axis=1, tiled=True)  6.61 us
    ppermute x2, starting transfers between devices, passed_along(): return lax.ppermute(value, axis, pairs)  5.95 us
    convert_element_type x2, local copies, waits for them, and re-layouts, cross_stack(): scaled.reshape(scaled.shape[0], 2, half_width * half_width)  5.55 us
    dot_general x2, matrix products, cross_stack(): jnp.einsum('fwa,fwb->fab', local_block, partner_block, preferred_element_...  5.35 us
  transfers between devices with their start and end apart: 4, of which 2 were waited for; matrix products, arithmetic and copies ran while one was open for 30% of the time, Pallas kernels for 0%

commit v1 on v0

v1 whole, which is shorter than its diff:
```python
import functools
import math

import jax
import jax.numpy as jnp
from jax import lax
from jax.experimental import pallas as pl
from jax.experimental.pallas import tpu as pltpu
from jax.sharding import PartitionSpec as P

ROUNDS = 2
CHUNKS = 2
PIECES = 2
RUN = 4
LANES = 128
MESH = pl.DeviceIdType.MESH
F32 = jnp.float32
BF16 = jnp.bfloat16


def stack_kernel(
    rows_y, rows_z, spectra, weight, out, held, table, weights, work, packed, relay, landed, sorted_, total,
    x_send, x_recv, y_send, y_recv, z_send, z_recv, row_send, row_recv,
):
    grp, frq = lax.axis_index("grp"), lax.axis_index("frq")
    y, xh, core = grp // 4, (grp // 2) % 2, grp % 2
    z, xl = frq // 2, frq % 2

    def device(y_, xh_, core_, z_, xl_):
        return (y_ * 4 + xh_ * 2 + core_, z_ * 2 + xl_)

    up, down = (y + 1) % rows_y, (y + rows_y - 1) % rows_y
    row = [(e, a, b) for e in range(2) for a in range(2) for b in range(2)]

    def in_row(e, a, b):
        return device(y, (xh + e) % 2, (core + b) % 2, z, (xl + a) % 2)

    barrier = pltpu.get_barrier_semaphore()
    partners = [in_row(*rel) for rel in row[1:]]
    partners += [device(y, xh, core, (z + k) % rows_z, xl) for k in range(1, rows_z)]
    partners += [device(up, xh, core, z, xl), device(down, xh, core, z, xl)]
    for partner in partners:
        pl.semaphore_signal(barrier, inc=1, device_id=partner, device_id_type=MESH)
    pl.semaphore_wait(barrier, len(partners))

    part = RUN // PIECES
    x_copies = []
    for n in range(CHUNKS):
        for p in range(PIECES):
            for e in range(2):
                for b in range(2):
                    to_xh, to_core = (xh + e) % 2, (core + b) % 2
                    first = n * 4 * RUN + RUN * (2 * to_xh + to_core) + part * p
                    copy = pltpu.make_async_remote_copy(
                        src_ref=spectra.at[0, pl.ds(first, part)],
                        dst_ref=held.at[2 + 2 * xh + core, pl.ds(n * RUN + part * p, part)],
                        send_sem=x_send.at[n, p, 2 * e + b],
                        recv_sem=x_recv.at[n, p, 2 * e + b],
                        device_id=device(y, to_xh, to_core, z, 1 - xl),
                        device_id_type=MESH,
                    )
                    copy.start()
                    x_copies.append(copy)

    def wait_x(n, p):
        for e in range(2):
            for b in range(2):
                slot = 2 + 2 * ((xh + e) % 2) + (core + b) % 2
                here = held.at[slot, pl.ds(n * RUN + part * p, part)]
                pltpu.make_async_copy(here, here, x_recv.at[n, p, 2 * e + b]).wait()

    def y_copy(n, p):
        return pltpu.make_async_remote_copy(
            src_ref=held.at[pl.ds(4, 2), pl.ds(n * RUN + part * p, part)],
            dst_ref=held.at[pl.ds(0, 2), pl.ds(n * RUN + part * p, part)],
            send_sem=y_send.at[n, p],
            recv_sem=y_recv.at[n, p],
            device_id=device(up, xh, core, z, xl),
            device_id_type=MESH,
        )

    def forward(n):
        for p in range(PIECES):
            wait_x(n, p)
            y_copy(n, p).start()

    lags = table.shape[2]
    bins = lags // 2
    for b in range(bins // LANES):
        wide = jnp.broadcast_to(weight[b : b + 1, :], (LANES, LANES))
        weights[pl.ds(b * LANES, LANES), :] = wide.T * (1.0 / math.sqrt(bins))

    group_rows = lax.broadcasted_iota(jnp.int32, (8, LANES), 0)
    group_cols = lax.broadcasted_iota(jnp.int32, (8, LANES), 1)
    turn = 2.0 * math.pi / lags
    steps = []
    for s in range(lags // LANES):
        angle = ((group_rows * (s * LANES)) % lags).astype(F32) * turn
        steps.append((jnp.cos(angle), jnp.sin(angle)))

    def table_rows(index, carry):
        n, group = index // (4 * rows_z), index % (4 * rows_z)
        hi, lo, depth = group // (2 * rows_z), (group // rows_z) % 2, group % rows_z
        first = pl.multiple_of(depth * 64 + (1 - lo) * 32 + n * 16 + hi * 8, 8)
        angle = (((group_rows + first) * group_cols) % lags).astype(F32) * turn
        scale = weights[pl.ds(first, 8), :]
        base_cos, base_sin = jnp.cos(angle) * scale, jnp.sin(angle) * scale
        at = pl.multiple_of(group * 16, 16)
        for s, (step_cos, step_sin) in enumerate(steps):
            real = base_cos * step_cos - base_sin * step_sin
            imag = base_sin * step_cos + base_cos * step_sin
            table[n, pl.ds(at, 16), s * LANES : (s + 1) * LANES] = jnp.concatenate([real, -imag], 0).astype(BF16)
        return carry

    lax.fori_loop(0, CHUNKS * 4 * rows_z, table_rows, 0)

    windows, width = held.shape[2], held.shape[3]
    half = width // 2
    tiles = packed.shape[5] // LANES
    lane = lax.broadcasted_iota(jnp.int32, (8, LANES), 1)
    sign = jnp.where(lax.broadcasted_iota(jnp.int32, (half, width), 1) < half, 1.0, -1.0)

    def products(n, m, c_to):
        hi = m // 2

        def one(f, carry):
            at = n * RUN + f
            pair = jnp.concatenate([held[m + 1, at], held[m, at]], 1)
            product = lax.dot_general(
                held[m + 2, at], pair, (((0,), (0,)), ((), ())), preferred_element_type=F32
            ) * (1.0 / math.sqrt(windows))
            for r in range(ROUNDS):
                block = product[:, r * width : (r + 1) * width]
                both = block[:half] * sign + pltpu.roll(block[half:], half, 1)
                work[pl.ds(pl.multiple_of((r * RUN + f) * half, half), half), :] = both
            return carry

        lax.fori_loop(0, RUN, one, 0, unroll=True)
        for pair in range(half // 2):
            first = work[pl.ds(2 * pair, 8, stride=half), :]
            second = work[pl.ds(2 * pair + 1, 8, stride=half), :]
            real = jnp.where(lane < half, first, pltpu.roll(second, half, 1))
            imag = jnp.where(lane < half, pltpu.roll(first, half, 1), second)
            depth, rest = pair // (2 * tiles), pair % (2 * tiles)
            lo, tile = rest // tiles, rest % tiles
            packed[2 * n + hi, depth, c_to, lo, :, tile * LANES : (tile + 1) * LANES] = jnp.concatenate(
                [real, imag], 0
            ).astype(BF16)

    def wave(n, hi):
        for c_to in range(2):
            products(n, 2 * hi + c_to, c_to)

    def z_copy(n, hi, k):
        w = 2 * n + hi
        return pltpu.make_async_remote_copy(
            src_ref=packed.at[w, (z + k) % rows_z],
            dst_ref=relay.at[w, z],
            send_sem=z_send.at[w, k],
            recv_sem=z_recv.at[w, k],
            device_id=device(y, xh, core, (z + k) % rows_z, xl),
            device_id_type=MESH,
        )

    def own_copy(n, hi):
        w = 2 * n + hi
        return pltpu.make_async_copy(packed.at[w, z], relay.at[w, z], z_recv.at[w, 0])

    def send_z(n, hi):
        for k in range(1, rows_z):
            z_copy(n, hi, k).start()
        own_copy(n, hi).start()

    def wait_z(n, hi):
        w = 2 * n + hi
        for k in range(rows_z):
            here = relay.at[w, (z + rows_z - k) % rows_z]
            pltpu.make_async_copy(here, here, z_recv.at[w, k]).wait()

    def row_copy(n, hi, e, a, b):
        w = 2 * n + hi
        return pltpu.make_async_remote_copy(
            src_ref=relay.at[w, :, (core + b) % 2, (xl + a) % 2],
            dst_ref=landed.at[n, 4 * xh + 2 * xl + core],
            send_sem=row_send.at[n, 4 * e + 2 * a + b],
            recv_sem=row_recv.at[n, 4 * e + 2 * a + b],
            device_id=device(y, hi, (core + b) % 2, z, (xl + a) % 2),
            device_id_type=MESH,
        )

    def send_row(n, hi):
        for e in range(2):
            @pl.when((xh + e) % 2 == hi)
            def _():
                for a in range(2):
                    for b in range(2):
                        if (e, a, b) == (0, 0, 0):
                            pltpu.make_async_copy(
                                relay.at[2 * n + hi, :, core, xl],
                                landed.at[n, 4 * xh + 2 * xl + core],
                                row_recv.at[n, 0],
                            ).start()
                        else:
                            row_copy(n, hi, e, a, b).start()

    def wait_row(n):
        for k, (e, a, b) in enumerate(row):
            here = landed.at[n, 4 * ((xh + e) % 2) + 2 * ((xl + a) % 2) + (core + b) % 2]
            pltpu.make_async_copy(here, here, row_recv.at[n, k]).wait()

    pairs = landed.shape[4]
    upper = lax.broadcasted_iota(jnp.int32, (8, pairs), 0) < RUN

    def sort(n):
        def one(group, carry):
            source, depth = group // rows_z, group % rows_z
            first = landed[n, 2 * source, depth].astype(F32)
            second = landed[n, 2 * source + 1, depth].astype(F32)
            kept, moved = [], []
            for c in range(2):
                a, b = first[8 * c : 8 * c + 8], second[8 * c : 8 * c + 8]
                kept.append(jnp.where(upper, a, pltpu.roll(b, RUN, 0)))
                moved.append(jnp.where(upper, pltpu.roll(a, RUN, 0), b))
            at = pl.multiple_of(group * 16, 16)
            sorted_[n, 0, pl.ds(at, 16), :] = jnp.concatenate(kept, 0).astype(BF16)
            sorted_[n, 1, pl.ds(at, 16), :] = jnp.concatenate(moved, 0).astype(BF16)
            return carry

        lax.fori_loop(0, 4 * rows_z, one, 0)

    def lag_product(n):
        step = min(256, lags)

        def one(index, carry):
            r, at = index // (lags // step), pl.multiple_of(index % (lags // step) * step, step)
            value = lax.dot_general(
                sorted_[n, r], table[n, :, pl.ds(at, step)], (((0,), (0,)), ((), ())), preferred_element_type=F32
            )
            if n == 0:
                total[r, :, pl.ds(at, step)] = value
            else:
                out[r, 0, :, pl.ds(at, step)] = (total[r, :, pl.ds(at, step)] + value).astype(BF16)
            return carry

        lax.fori_loop(0, ROUNDS * (lags // step), one, 0)

    def wait_y(n):
        for p in range(PIECES):
            y_copy(n, p).wait_recv()

    forward(0)
    wave(0, 1)
    send_z(0, 1)
    wait_y(0)
    wave(0, 0)
    send_z(0, 0)
    forward(1)
    wave(1, 1)
    send_z(1, 1)
    wait_z(0, 1)
    send_row(0, 1)
    wait_z(0, 0)
    send_row(0, 0)
    wait_y(1)
    wave(1, 0)
    send_z(1, 0)
    wait_z(1, 1)
    send_row(1, 1)
    wait_row(0)
    sort(0)
    lag_product(0)
    wait_z(1, 0)
    send_row(1, 0)
    wait_row(1)
    sort(1)
    lag_product(1)

    for copy in x_copies:
        copy.wait_send()
    for n in range(CHUNKS):
        for p in range(PIECES):
            y_copy(n, p).wait_send()
        for hi in range(2):
            for k in range(1, rows_z):
                z_copy(n, hi, k).wait_send()
            for e in range(2):
                @pl.when((xh + e) % 2 == hi)
                def _():
                    for a in range(2):
                        for b in range(2):
                            if (e, a, b) != (0, 0, 0):
                                row_copy(n, hi, e, a, b).wait_send()


def local(rows_y, rows_z, spectra, band_weight):
    _, freqs, windows, width = spectra.shape
    bins = band_weight.shape[0]
    lags = 2 * bins
    pairs = (width // 2) ** 2 // (2 * rows_z)
    held_freqs = CHUNKS * RUN
    rows = 4 * rows_z * 16
    dma = pltpu.SemaphoreType.DMA
    return pl.pallas_call(
        functools.partial(stack_kernel, rows_y, rows_z),
        name="stack",
        out_shape=jax.ShapeDtypeStruct((ROUNDS, 1, pairs, lags), BF16),
        in_specs=[pl.BlockSpec(memory_space=pl.ANY), pl.BlockSpec(memory_space=pltpu.VMEM)],
        out_specs=pl.BlockSpec(memory_space=pltpu.VMEM),
        scratch_shapes=[
            pltpu.VMEM((6, held_freqs, windows, width), BF16),
            pltpu.VMEM((CHUNKS, rows, lags), BF16),
            pltpu.VMEM((bins, LANES), F32),
            pltpu.VMEM((ROUNDS * RUN * width // 2, width), F32),
            pltpu.VMEM((2 * CHUNKS, rows_z, 2, 2, 16, pairs), BF16),
            pltpu.VMEM((2 * CHUNKS, rows_z, 2, 2, 16, pairs), BF16),
            pltpu.VMEM((CHUNKS, 8, rows_z, 16, pairs), BF16),
            pltpu.VMEM((CHUNKS, ROUNDS, rows, pairs), BF16),
            pltpu.VMEM((ROUNDS, pairs, lags), F32),
            dma((CHUNKS, PIECES, 4)),
            dma((CHUNKS, PIECES, 4)),
            dma((CHUNKS, PIECES)),
            dma((CHUNKS, PIECES)),
            dma((2 * CHUNKS, rows_z)),
            dma((2 * CHUNKS, rows_z)),
            dma((CHUNKS, 8)),
            dma((CHUNKS, 8)),
        ],
        compiler_params=pltpu.CompilerParams(
            collective_id=0, has_side_effects=True, vmem_limit_bytes=40 * 2**20
        ),
    )(spectra, band_weight.reshape(bins // LANES, LANES))


def solution(mesh):
    rows_y, rows_z = mesh.shape["grp"] // 4, mesh.shape["frq"] // 2
    return jax.shard_map(
        functools.partial(local, rows_y, rows_z),
        mesh=mesh,
        in_specs=(P("grp", "frq", None, None), P()),
        out_specs=P(None, "grp", "frq", None),
        check_vma=False,
    )
```

time: 123 us -> 70.5 us (0.57)
  the two profiles are of different devices: /device:TPU:2 before, /device:TPU:1 now
where the time goes in v1:
time: 70.5 us; the launch traced here: 70.3 us
  Pallas kernels  67.1 us (95%)
  local copies, waits for them, and re-layouts  3.2 us (5%)
    pallas_call x1, Pallas kernels, local(): pl.pallas_call(functools.partial(stack_kernel, rows_y, rows_z), name='sta...  67.1 us
    unnamed x5, local copies, waits for them, and re-layouts  3.2 us

profile of v1, /device:TPU:1, one launch (start us, length us, event | category | flops | bytes accessed | tf_op | source)
XLA Modules:
  0.0 70.3 jit_solution(4538260953279860315)
XLA Ops:
  0.0 0.0 copy-start
  0.0 1.5 %copy-done = bf16[1,32,240,128]{3,2,1,0:T(8,128)(2,1)S(1)} copy-done((bf16[1,32,240,128]{3,2,1,0:T(8,128)(2,1)S(1)}, bf16[1,32,240,128]{3,2,1,0:T(8,128)(2,1)}, u32[]{:S(2)}) %copy-start) | copy-done | bytes 1966104
  1.5 0.0 copy-start.1
  1.5 0.7 copy-done.1
  2.2 67.1 %stack.1 = bf16[2,1,256,1024]{3,2,1,0:T(8,128)(2,1)S(1)} custom-call(bf16[1,32,240,128]{3,2,1,0:T(8,128)(2,1)S(1)} %copy-done, f32[4,128]{1,0:T(4,128)S(1)} %bitcast.1), custom_call_target="tpu_custom_call" | custom-call | tf_op jit(solution)/shard_map/stack/pallas_call | solution.py:303
  69.4 1.0 %copy.4 = bf16[2,1,256,1024]{3,2,1,0:T(8,128)(2,1)} copy(bf16[2,1,256,1024]{3,2,1,0:T(8,128)(2,1)S(1)} %stack.1) | data formatting | bytes 2097152
Async XLA Ops:
  0.0 1.5 %copy-start = (bf16[1,32,240,128]{3,2,1,0:T(8,128)(2,1)S(1)}, bf16[1,32,240,128]{3,2,1,0:T(8,128)(2,1)}, u32[]{:S(2)}) copy-start(bf16[1,32,240,128]{3,2,1,0:T(8,128)(2,1)} %spectra.1) | copy-start | bytes 5898244
  1.5 0.7 copy-start.1

commit v2 on v1

v2 whole, which is shorter than its diff:
```python
import functools
import math

import jax
import jax.numpy as jnp
from jax import lax
from jax.experimental import pallas as pl
from jax.experimental.pallas import tpu as pltpu
from jax.sharding import PartitionSpec as P

ROUNDS = 2
CHUNKS = 4
RUN = 2
LANES = 128
MESH = pl.DeviceIdType.MESH
F32 = jnp.float32
BF16 = jnp.bfloat16


def stack_kernel(
    rows_y, rows_z, spectra, weight_in, out, weight, held, table, weights, work, packed, relay, landed, sorted_, total,
    x_send, x_recv, y_send, y_recv, z_send, z_recv, row_send, row_recv, direct_send, direct_recv, own_sem,
):
    grp, frq = lax.axis_index("grp"), lax.axis_index("frq")
    y, xh, core = grp // 4, (grp // 2) % 2, grp % 2
    z, xl = frq // 2, frq % 2

    def device(y_, xh_, core_, z_, xl_):
        return (y_ * 4 + xh_ * 2 + core_, z_ * 2 + xl_)

    up, down = (y + 1) % rows_y, (y + rows_y - 1) % rows_y
    row = [(e, a, b) for e in range(2) for a in range(2) for b in range(2)]

    def in_plane(k, e, a, b):
        return device(y, (xh + e) % 2, (core + b) % 2, (z + k) % rows_z, (xl + a) % 2)

    windows, width = held.shape[2], held.shape[3]
    whole, halves = [(0, windows)], [(0, LANES), (LANES, windows - LANES)]
    pieces = [
        [(n * RUN + f, *cut) for f in range(RUN) for cut in (halves if n == CHUNKS - 1 else whole)]
        for n in range(CHUNKS)
    ]

    barrier = pltpu.get_barrier_semaphore()
    plane = [(k, *rel) for k in range(rows_z) for rel in row]
    partners = [in_plane(*rel) for rel in plane[1:]]
    partners += [device(up, xh, core, z, xl), device(down, xh, core, z, xl)]
    for partner in partners:
        pl.semaphore_signal(barrier, inc=1, device_id=partner, device_id_type=MESH)
    pl.semaphore_wait(barrier, len(partners))

    weight_copy = pltpu.make_async_copy(weight_in, weight, own_sem)
    weight_copy.start()

    x_copies = []
    for n in range(CHUNKS):
        for p, (f, row_first, row_count) in enumerate(pieces[n]):
            for e in range(2):
                for b in range(2):
                    to_xh, to_core = (xh + e) % 2, (core + b) % 2
                    source = n * 3 * RUN + RUN * (2 * to_xh + to_core) + f
                    copy = pltpu.make_async_remote_copy(
                        src_ref=spectra.at[0, source, pl.ds(row_first, row_count)],
                        dst_ref=held.at[2 + 2 * xh + core, f, pl.ds(row_first, row_count)],
                        send_sem=x_send.at[n, p, 2 * e + b],
                        recv_sem=x_recv.at[n, p, 2 * e + b],
                        device_id=device(y, to_xh, to_core, z, 1 - xl),
                        device_id_type=MESH,
                    )
                    copy.start()
                    x_copies.append(copy)

    def wait_x(n, p):
        f, row_first, row_count = pieces[n][p]
        for e in range(2):
            for b in range(2):
                slot = 2 + 2 * ((xh + e) % 2) + (core + b) % 2
                here = held.at[slot, f, pl.ds(row_first, row_count)]
                pltpu.make_async_copy(here, here, x_recv.at[n, p, 2 * e + b]).wait()

    def y_copy(n, p):
        f, row_first, row_count = pieces[n][p]
        return pltpu.make_async_remote_copy(
            src_ref=held.at[pl.ds(4, 2), f, pl.ds(row_first, row_count)],
            dst_ref=held.at[pl.ds(0, 2), f, pl.ds(row_first, row_count)],
            send_sem=y_send.at[n, p],
            recv_sem=y_recv.at[n, p],
            device_id=device(up, xh, core, z, xl),
            device_id_type=MESH,
        )

    def forward(n, p):
        wait_x(n, p)
        y_copy(n, p).start()

    lags = table.shape[1]
    bins = lags // 2
    weight_copy.wait()
    for b in range(bins // LANES):
        wide = jnp.broadcast_to(weight[b : b + 1, :], (LANES, LANES))
        weights[pl.ds(b * LANES, LANES), :] = wide.T * (1.0 / math.sqrt(bins))

    group_rows = lax.broadcasted_iota(jnp.int32, (8, LANES), 0)
    group_cols = lax.broadcasted_iota(jnp.int32, (8, LANES), 1)
    turn = 2.0 * math.pi / lags
    steps = []
    for s in range(lags // LANES):
        angle = ((group_rows * (s * LANES)) % lags).astype(F32) * turn
        steps.append((jnp.cos(angle), jnp.sin(angle)))

    def table_rows(index, carry):
        n, group = index // (2 * rows_z), index % (2 * rows_z)
        lo, depth = group // rows_z, group % rows_z
        first = pl.multiple_of(depth * 64 + (1 - lo) * 32 + n * 8, 8)
        angle = (((group_rows + first) * group_cols) % lags).astype(F32) * turn
        scale = weights[pl.ds(first, 8), :]
        base_cos, base_sin = jnp.cos(angle) * scale, jnp.sin(angle) * scale
        at = pl.multiple_of(index * 16, 16)
        for s, (step_cos, step_sin) in enumerate(steps):
            real = base_cos * step_cos - base_sin * step_sin
            imag = base_sin * step_cos + base_cos * step_sin
            table[pl.ds(at, 16), s * LANES : (s + 1) * LANES] = jnp.concatenate([real, -imag], 0).astype(BF16)
        return carry

    lax.fori_loop(0, CHUNKS * 2 * rows_z, table_rows, 0)

    half = width // 2
    lane = lax.broadcasted_iota(jnp.int32, (8, LANES), 1) < half
    sublane = lax.broadcasted_iota(jnp.int32, (8, LANES), 0)
    sign = jnp.where(lax.broadcasted_iota(jnp.int32, (half, width), 1) < half, 1.0, -1.0)

    def products(n, hi):
        for c_to in range(2):
            m = 2 * hi + c_to
            for f in range(RUN):
                at = n * RUN + f
                pair = jnp.concatenate([held[m + 1, at], held[m, at]], 1)
                product = lax.dot_general(
                    held[m + 2, at], pair, (((0,), (0,)), ((), ())), preferred_element_type=F32
                ) * (1.0 / math.sqrt(windows))
                for r in range(ROUNDS):
                    block = product[:, r * width : (r + 1) * width]
                    both = block[:half] * sign + pltpu.roll(block[half:], half, 1)
                    work[pl.ds(((c_to * ROUNDS + r) * RUN + f) * half, half), :] = both
        for shard in range(half // 4):
            real, imag = [], []
            for h in range(2):
                first = work[pl.ds(4 * shard + 2 * h, 8, stride=half), :]
                second = work[pl.ds(4 * shard + 2 * h + 1, 8, stride=half), :]
                real.append(jnp.where(lane, first, pltpu.roll(second, half, 1)))
                imag.append(jnp.where(lane, pltpu.roll(first, half, 1), second))
            for c_to in range(2):
                parts = []
                for lower, upper in (real, imag):
                    if c_to:
                        lower = pltpu.roll(lower, 4, 0)
                    else:
                        upper = pltpu.roll(upper, 4, 0)
                    parts.append(jnp.where(sublane < 4, lower, upper))
                packed[2 * n + hi, shard // 2, c_to, shard % 2] = jnp.concatenate(parts, 0).astype(BF16)

    last = CHUNKS - 1
    far_first = sorted(range(1, rows_z), key=lambda k: -min(k, rows_z - k))

    def z_copy(n, hi, k):
        w = 2 * n + hi
        return pltpu.make_async_remote_copy(
            src_ref=packed.at[w, (z + k) % rows_z],
            dst_ref=relay.at[w, z],
            send_sem=z_send.at[w, k],
            recv_sem=z_recv.at[w, k],
            device_id=device(y, xh, core, (z + k) % rows_z, xl),
            device_id_type=MESH,
        )

    def wave(n, hi):
        products(n, hi)
        for k in far_first:
            z_copy(n, hi, k).start()
        w = 2 * n + hi
        pltpu.make_async_copy(packed.at[w, z], relay.at[w, z], z_recv.at[w, 0]).start()

    def wait_z(n, hi):
        w = 2 * n + hi
        for k in range(rows_z):
            here = relay.at[w, (z + rows_z - k) % rows_z]
            pltpu.make_async_copy(here, here, z_recv.at[w, k]).wait()

    own_source = 4 * xh + 2 * xl + core

    def row_copy(n, hi, a, b):
        return pltpu.make_async_remote_copy(
            src_ref=relay.at[2 * n + hi, :, (core + b) % 2, (xl + a) % 2],
            dst_ref=landed.at[n, own_source],
            send_sem=row_send.at[n, hi, 2 * a + b],
            recv_sem=row_recv.at[n, 4 * ((xh + hi) % 2) + 2 * a + b],
            device_id=device(y, hi, (core + b) % 2, z, (xl + a) % 2),
            device_id_type=MESH,
        )

    def send_row(n, hi):
        wait_z(n, hi)
        for a, b in ((1, 0), (1, 1), (0, 1)):
            row_copy(n, hi, a, b).start()

        @pl.when(xh != hi)
        def _():
            row_copy(n, hi, 0, 0).start()

        @pl.when(xh == hi)
        def _():
            pltpu.make_async_copy(
                relay.at[2 * n + hi, :, core, xl], landed.at[n, own_source], row_recv.at[n, 0]
            ).start()

    def direct_copy(hi, k, a, b):
        to_z, to_core, to_xl = (z + k) % rows_z, (core + b) % 2, (xl + a) % 2
        return pltpu.make_async_remote_copy(
            src_ref=packed.at[2 * last + hi, to_z, to_core, to_xl],
            dst_ref=landed.at[last, own_source, z],
            send_sem=direct_send.at[hi, k, 2 * a + b],
            recv_sem=direct_recv,
            device_id=device(y, hi, to_core, to_z, to_xl),
            device_id_type=MESH,
        )

    def direct(hi):
        products(last, hi)
        for k in far_first:
            for a in range(2):
                for b in range(2):
                    direct_copy(hi, k, a, b).start()
        for a, b in ((1, 0), (1, 1), (0, 1)):
            direct_copy(hi, 0, a, b).start()

        @pl.when(xh != hi)
        def _():
            direct_copy(hi, 0, 0, 0).start()

        @pl.when(xh == hi)
        def _():
            pltpu.make_async_copy(
                packed.at[2 * last + hi, z, core, xl], landed.at[last, own_source, z], direct_recv
            ).start()

    def wait_direct():
        pltpu.make_async_copy(landed.at[last], landed.at[last], direct_recv).wait()

    def wait_row(n):
        for k, (e, a, b) in enumerate(row):
            here = landed.at[n, 4 * ((xh + e) % 2) + 2 * ((xl + a) % 2) + (core + b) % 2]
            pltpu.make_async_copy(here, here, row_recv.at[n, k]).wait()

    span = 2 * rows_z * 16

    def sort(n):
        def one(group, carry):
            lo, depth = group // rows_z, group % rows_z
            tiles = [landed[n, 4 * (s // 2) + 2 * lo + s % 2, depth].astype(F32) for s in range(4)]
            at = pl.multiple_of(n * span + group * 16, 16)
            for h in range(2):
                for r in range(ROUNDS):
                    parts = []
                    for c in range(2):
                        value = None
                        for s in range(4):
                            turned = tiles[s][8 * c : 8 * c + 8]
                            amount = 2 * (s - (2 * h + r)) % 8
                            if amount:
                                turned = pltpu.roll(turned, amount, 0)
                            value = turned if value is None else jnp.where(sublane < 2 * s, value, turned)
                        parts.append(value)
                    sorted_[r, pl.ds(at, 16), h * LANES : (h + 1) * LANES] = jnp.concatenate(parts, 0).astype(BF16)
            return carry

        lax.fori_loop(0, 2 * rows_z, one, 0)

    def lag_product(first, stop):
        rows = pl.ds(first * span, (stop - first) * span)

        def one(r, carry):
            value = lax.dot_general(
                sorted_[r, rows, :], table[rows, :], (((0,), (0,)), ((), ())), preferred_element_type=F32
            )
            if stop < CHUNKS:
                total[r] = value
            else:
                out[r, 0] = (total[r] + value).astype(BF16)
            return carry

        lax.fori_loop(0, ROUNDS, one, 0)

    def wait_y(n):
        for p in range(len(pieces[n])):
            y_copy(n, p).wait_recv()

    for p in range(len(pieces[0])):
        forward(0, p)
    wave(0, 1)
    for n in range(last):
        half_way = len(pieces[n + 1]) // 2
        for p in range(half_way):
            forward(n + 1, p)
        wait_y(n)
        wave(n, 0)
        for p in range(half_way, len(pieces[n + 1])):
            forward(n + 1, p)
        if n + 1 < last:
            wave(n + 1, 1)
    direct(1)
    for n in range(last):
        for hi in (1, 0):
            send_row(n, hi)
    wait_y(last)
    direct(0)
    for n in range(last):
        wait_row(n)
        sort(n)
    lag_product(0, last)
    wait_direct()
    sort(last)
    lag_product(last, CHUNKS)

    for copy in x_copies:
        copy.wait_send()
    for n in range(CHUNKS):
        for p in range(len(pieces[n])):
            y_copy(n, p).wait_send()
    for hi in range(2):
        for n in range(last):
            for k in range(1, rows_z):
                z_copy(n, hi, k).wait_send()
            for a, b in ((1, 0), (1, 1), (0, 1)):
                row_copy(n, hi, a, b).wait_send()
        for k in range(rows_z):
            for a in range(2):
                for b in range(2):
                    if (k, a, b) != (0, 0, 0):
                        direct_copy(hi, k, a, b).wait_send()

        @pl.when(xh != hi)
        def _():
            direct_copy(hi, 0, 0, 0).wait_send()
            for n in range(last):
                row_copy(n, hi, 0, 0).wait_send()


def in_hbm(array):
    return pltpu.with_memory_space_constraint(array, pltpu.HBM)


def local(rows_y, rows_z, spectra, band_weight):
    _, freqs, windows, width = spectra.shape
    bins = band_weight.shape[0]
    lags = 2 * bins
    pairs = (width // 2) ** 2 // (2 * rows_z)
    held_freqs = CHUNKS * RUN
    rows = CHUNKS * 2 * rows_z * 16
    dma = pltpu.SemaphoreType.DMA
    return pl.pallas_call(
        functools.partial(stack_kernel, rows_y, rows_z),
        name="stack",
        out_shape=jax.ShapeDtypeStruct((ROUNDS, 1, pairs, lags), BF16),
        in_specs=[pl.BlockSpec(memory_space=pltpu.HBM), pl.BlockSpec(memory_space=pltpu.HBM)],
        out_specs=pl.BlockSpec(memory_space=pltpu.VMEM),
        scratch_shapes=[
            pltpu.VMEM((bins // LANES, LANES), F32),
            pltpu.VMEM((6, held_freqs, windows, width), BF16),
            pltpu.VMEM((rows, lags), BF16),
            pltpu.VMEM((bins, LANES), F32),
            pltpu.VMEM((2 * ROUNDS * RUN * width // 2, width), F32),
            pltpu.VMEM((2 * CHUNKS, rows_z, 2, 2, 16, LANES), BF16),
            pltpu.VMEM((2 * CHUNKS, rows_z, 2, 2, 16, LANES), BF16),
            pltpu.VMEM((CHUNKS, 8, rows_z, 16, LANES), BF16),
            pltpu.VMEM((ROUNDS, rows, pairs), BF16),
            pltpu.VMEM((ROUNDS, pairs, lags), F32),
            dma((CHUNKS, 2 * RUN, 4)),
            dma((CHUNKS, 2 * RUN, 4)),
            dma((CHUNKS, 2 * RUN)),
            dma((CHUNKS, 2 * RUN)),
            dma((2 * CHUNKS, rows_z)),
            dma((2 * CHUNKS, rows_z)),
            dma((CHUNKS, 2, 4)),
            dma((CHUNKS, 8)),
            dma((2, rows_z, 4)),
            dma,
            dma,
        ],
        compiler_params=pltpu.CompilerParams(
            collective_id=0, has_side_effects=True, vmem_limit_bytes=48 * 2**20
        ),
    )(in_hbm(spectra), in_hbm(band_weight.reshape(bins // LANES, LANES)))


def solution(mesh):
    rows_y, rows_z = mesh.shape["grp"] // 4, mesh.shape["frq"] // 2
    return jax.shard_map(
        functools.partial(local, rows_y, rows_z),
        mesh=mesh,
        in_specs=(P("grp", "frq", None, None), P()),
        out_specs=P(None, "grp", "frq", None),
        check_vma=False,
    )
```

time: 70.5 us -> 62 us (0.88)
  Pallas kernels: 67.1 us -> 60.9 us
  local copies, waits for them, and re-layouts: 3.2 us -> 0.97 us
    pallas_call x1, Pallas kernels: 67.1 us -> 60.9 us  [local(): pl.pallas_call(functools.partial(stack_kernel, rows_y, rows_z), name='sta...]
    unnamed x5 -> x1, local copies, waits for them, and re-layouts: 3.2 us -> 0.97 us
where the time goes in v2:
time: 62 us; the launch traced here: 61.8 us
  Pallas kernels  60.9 us (98%)
  local copies, waits for them, and re-layouts  0.97 us (2%)
    pallas_call x1, Pallas kernels, local(): pl.pallas_call(functools.partial(stack_kernel, rows_y, rows_z), name='sta...  60.9 us

profile of v2, /device:TPU:1, one launch (start us, length us, event | category | flops | bytes accessed | tf_op | source)
XLA Modules:
  0.0 61.8 jit_solution(12978150982690920502)
XLA Ops:
  0.0 60.9 %stack.1 = bf16[2,1,256,1024]{3,2,1,0:T(8,128)(2,1)S(1)} custom-call(bf16[1,32,240,128]{3,2,1,0:T(8,128)(2,1)} %spectra.1, f32[4,128]{1,0:T(4,128)} %bitcast.1), custom_call_target="tpu_custom_call" | custom-call | tf_op jit(solution)/shard_map/stack/pallas_call | solution.py:360
  60.9 1.0 %copy.4 = bf16[2,1,256,1024]{3,2,1,0:T(8,128)(2,1)} copy(bf16[2,1,256,1024]{3,2,1,0:T(8,128)(2,1)S(1)} %stack.1) | data formatting | bytes 2097152

commit v3 on v2

--- a/solution.py
+++ b/solution.py
@@ -19,7 +19,7 @@
 
 def stack_kernel(
     rows_y, rows_z, spectra, weight_in, out, weight, held, table, weights, work, packed, relay, landed, sorted_, total,
-    x_send, x_recv, y_send, y_recv, z_send, z_recv, row_send, row_recv, direct_send, direct_recv, own_sem,
+    x_send, x_recv, y_send, y_recv, z_send, z_recv, row_send, row_recv, direct_send, direct_recv, own_sem, row_here, plane_here,
 ):
     grp, frq = lax.axis_index("grp"), lax.axis_index("frq")
     y, xh, core = grp // 4, (grp // 2) % 2, grp % 2
@@ -42,12 +42,27 @@
     ]
 
     barrier = pltpu.get_barrier_semaphore()
-    plane = [(k, *rel) for k in range(rows_z) for rel in row]
-    partners = [in_plane(*rel) for rel in plane[1:]]
-    partners += [device(up, xh, core, z, xl), device(down, xh, core, z, xl)]
-    for partner in partners:
-        pl.semaphore_signal(barrier, inc=1, device_id=partner, device_id_type=MESH)
-    pl.semaphore_wait(barrier, len(partners))
+    own_source = 4 * xh + 2 * xl + core
+    leads = own_source == 0
+
+    def say(semaphore, who):
+        pl.semaphore_signal(semaphore, inc=1, device_id=who, device_id_type=MESH)
+
+    for e, a, b in row[1:]:
+        @pl.when(4 * ((xh + e) % 2) + 2 * ((xl + a) % 2) + (core + b) % 2 != 0)
+        def _():
+            say(barrier, in_plane(0, e, a, b))
+    say(barrier, device(up, xh, core, z, xl))
+    say(barrier, device(down, xh, core, z, xl))
+
+    @pl.when(jnp.logical_not(leads))
+    def _():
+        pl.semaphore_wait(barrier, 9)
+        say(row_here, device(y, 0, 0, z, 0))
+
+    @pl.when(leads)
+    def _():
+        pl.semaphore_wait(row_here, 7)
 
     weight_copy = pltpu.make_async_copy(weight_in, weight, own_sem)
     weight_copy.start()
@@ -70,6 +85,11 @@
                     copy.start()
                     x_copies.append(copy)
 
+    @pl.when(leads)
+    def _():
+        for k in range(1, rows_z):
+            say(barrier, in_plane(k, 0, 0, 0))
+
     def wait_x(n, p):
         f, row_first, row_count = pieces[n][p]
         for e in range(2):
@@ -123,6 +143,12 @@
         return carry
 
     lax.fori_loop(0, CHUNKS * 2 * rows_z, table_rows, 0)
+
+    @pl.when(leads)
+    def _():
+        pl.semaphore_wait(barrier, 2 + rows_z - 1)
+        for e, a, b in row[1:]:
+            say(plane_here, in_plane(0, e, a, b))
 
     half = width // 2
     lane = lax.broadcasted_iota(jnp.int32, (8, LANES), 1) < half
@@ -173,20 +199,21 @@
             device_id_type=MESH,
         )
 
-    def wave(n, hi):
-        products(n, hi)
+    def send_z(n, hi):
         for k in far_first:
             z_copy(n, hi, k).start()
         w = 2 * n + hi
         pltpu.make_async_copy(packed.at[w, z], relay.at[w, z], z_recv.at[w, 0]).start()
+
+    def wave(n, hi):
+        products(n, hi)
+        send_z(n, hi)
 
     def wait_z(n, hi):
         w = 2 * n + hi
         for k in range(rows_z):
             here = relay.at[w, (z + rows_z - k) % rows_z]
             pltpu.make_async_copy(here, here, z_recv.at[w, k]).wait()
-
-    own_source = 4 * xh + 2 * xl + core
 
     def row_copy(n, hi, a, b):
         return pltpu.make_async_remote_copy(
@@ -296,21 +323,32 @@
 
     for p in range(len(pieces[0])):
         forward(0, p)
-    wave(0, 1)
+    products(0, 1)
+
+    @pl.when(jnp.logical_not(leads))
+    def _():
+        pl.semaphore_wait(plane_here, 1)
+
+    send_z(0, 1)
     for n in range(last):
         half_way = len(pieces[n + 1]) // 2
         for p in range(half_way):
             forward(n + 1, p)
         wait_y(n)
         wave(n, 0)
+        if n + 1 == last:
+            pass
+            send_row(0, 1)
+            send_row(0, 0)
+            send_row(1, 1)
+            send_row(1, 0)
         for p in range(half_way, len(pieces[n + 1])):
             forward(n + 1, p)
         if n + 1 < last:
             wave(n + 1, 1)
     direct(1)
-    for n in range(last):
-        for hi in (1, 0):
-            send_row(n, hi)
+    send_row(2, 1)
+    send_row(2, 0)
     wait_y(last)
     direct(0)
     for n in range(last):
@@ -385,6 +423,8 @@
             dma((2, rows_z, 4)),
             dma,
             dma,
+            pltpu.SemaphoreType.REGULAR,
+            pltpu.SemaphoreType.REGULAR,
         ],
         compiler_params=pltpu.CompilerParams(
             collective_id=0, has_side_effects=True, vmem_limit_bytes=48 * 2**20

time: 62 us -> 60.5 us (0.976)
  Pallas kernels: 60.9 us -> 59.4 us
    pallas_call x1, Pallas kernels: 60.9 us -> 59.4 us  [local(): pl.pallas_call(functools.partial(stack_kernel, rows_y, rows_z), name='sta...]
where the time goes in v3:
time: 60.5 us; the launch traced here: 60.4 us
  Pallas kernels  59.4 us (98%)
  local copies, waits for them, and re-layouts  0.97 us (2%)
    pallas_call x1, Pallas kernels, local(): pl.pallas_call(functools.partial(stack_kernel, rows_y, rows_z), name='sta...  59.4 us

profile of v3, /device:TPU:1, one launch (start us, length us, event | category | flops | bytes accessed | tf_op | source)
XLA Modules:
  0.0 60.4 jit_solution(2364434017343396011)
XLA Ops:
  0.0 59.4 %stack.1 = bf16[2,1,256,1024]{3,2,1,0:T(8,128)(2,1)S(1)} custom-call(bf16[1,32,240,128]{3,2,1,0:T(8,128)(2,1)} %spectra.1, f32[4,128]{1,0:T(4,128)} %bitcast.1), custom_call_target="tpu_custom_call" | custom-call | tf_op jit(solution)/shard_map/stack/pallas_call | solution.py:398
  59.4 1.0 %copy.4 = bf16[2,1,256,1024]{3,2,1,0:T(8,128)(2,1)} copy(bf16[2,1,256,1024]{3,2,1,0:T(8,128)(2,1)S(1)} %stack.1) | data formatting | bytes 2097152

commit v4 on v3

--- a/solution.py
+++ b/solution.py
@@ -11,6 +11,7 @@
 ROUNDS = 2
 CHUNKS = 4
 RUN = 2
+DIRECT = 2
 LANES = 128
 MESH = pl.DeviceIdType.MESH
 F32 = jnp.float32
@@ -186,6 +187,7 @@
                 packed[2 * n + hi, shard // 2, c_to, shard % 2] = jnp.concatenate(parts, 0).astype(BF16)
 
     last = CHUNKS - 1
+    relayed = CHUNKS - DIRECT
     far_first = sorted(range(1, rows_z), key=lambda k: -min(k, rows_z - k))
 
     def z_copy(n, hi, k):
@@ -205,10 +207,6 @@
         w = 2 * n + hi
         pltpu.make_async_copy(packed.at[w, z], relay.at[w, z], z_recv.at[w, 0]).start()
 
-    def wave(n, hi):
-        products(n, hi)
-        send_z(n, hi)
-
     def wait_z(n, hi):
         w = 2 * n + hi
         for k in range(rows_z):
@@ -240,38 +238,47 @@
                 relay.at[2 * n + hi, :, core, xl], landed.at[n, own_source], row_recv.at[n, 0]
             ).start()
 
-    def direct_copy(hi, k, a, b):
+    def direct_copy(n, hi, k, a, b):
         to_z, to_core, to_xl = (z + k) % rows_z, (core + b) % 2, (xl + a) % 2
         return pltpu.make_async_remote_copy(
-            src_ref=packed.at[2 * last + hi, to_z, to_core, to_xl],
-            dst_ref=landed.at[last, own_source, z],
-            send_sem=direct_send.at[hi, k, 2 * a + b],
-            recv_sem=direct_recv,
+            src_ref=packed.at[2 * n + hi, to_z, to_core, to_xl],
+            dst_ref=landed.at[n, own_source, z],
+            send_sem=direct_send.at[n - relayed, hi, k, 2 * a + b],
+            recv_sem=direct_recv.at[n - relayed],
             device_id=device(y, hi, to_core, to_z, to_xl),
             device_id_type=MESH,
         )
 
-    def direct(hi):
-        products(last, hi)
+    def send_direct(n, hi):
         for k in far_first:
             for a in range(2):
                 for b in range(2):
-                    direct_copy(hi, k, a, b).start()
+                    direct_copy(n, hi, k, a, b).start()
         for a, b in ((1, 0), (1, 1), (0, 1)):
-            direct_copy(hi, 0, a, b).start()
+            direct_copy(n, hi, 0, a, b).start()
 
         @pl.when(xh != hi)
         def _():
-            direct_copy(hi, 0, 0, 0).start()
+            direct_copy(n, hi, 0, 0, 0).start()
 
         @pl.when(xh == hi)
         def _():
             pltpu.make_async_copy(
-                packed.at[2 * last + hi, z, core, xl], landed.at[last, own_source, z], direct_recv
+                packed.at[2 * n + hi, z, core, xl], landed.at[n, own_source, z], direct_recv.at[n - relayed]
             ).start()
 
-    def wait_direct():
-        pltpu.make_async_copy(landed.at[last], landed.at[last], direct_recv).wait()
+    def wait_direct(n):
+        pltpu.make_async_copy(landed.at[n], landed.at[n], direct_recv.at[n - relayed]).wait()
+
+    def send_wave(n, hi):
+        if n < relayed:
+            send_z(n, hi)
+        else:
+            send_direct(n, hi)
+
+    def wave(n, hi):
+        products(n, hi)
+        send_wave(n, hi)
 
     def wait_row(n):
         for k, (e, a, b) in enumerate(row):
@@ -329,7 +336,7 @@
     def _():
         pl.semaphore_wait(plane_here, 1)
 
-    send_z(0, 1)
+    send_wave(0, 1)
     for n in range(last):
         half_way = len(pieces[n + 1]) // 2
         for p in range(half_way):
@@ -337,25 +344,25 @@
         wait_y(n)
         wave(n, 0)
         if n + 1 == last:
-            pass
-            send_row(0, 1)
-            send_row(0, 0)
-            send_row(1, 1)
-            send_row(1, 0)
+            for early in range(min(2, relayed)):
+                for hi in (1, 0):
+                    send_row(early, hi)
         for p in range(half_way, len(pieces[n + 1])):
             forward(n + 1, p)
-        if n + 1 < last:
-            wave(n + 1, 1)
-    direct(1)
-    send_row(2, 1)
-    send_row(2, 0)
+        wave(n + 1, 1)
+    for early in range(2, relayed):
+        for hi in (1, 0):
+            send_row(early, hi)
     wait_y(last)
-    direct(0)
+    wave(last, 0)
     for n in range(last):
-        wait_row(n)
+        if n < relayed:
+            wait_row(n)
+        else:
+            wait_direct(n)
         sort(n)
     lag_product(0, last)
-    wait_direct()
+    wait_direct(last)
     sort(last)
     lag_product(last, CHUNKS)
 
@@ -364,23 +371,26 @@
     for n in range(CHUNKS):
         for p in range(len(pieces[n])):
             y_copy(n, p).wait_send()
-    for hi in range(2):
-        for n in range(last):
-            for k in range(1, rows_z):
-                z_copy(n, hi, k).wait_send()
-            for a, b in ((1, 0), (1, 1), (0, 1)):
-                row_copy(n, hi, a, b).wait_send()
-        for k in range(rows_z):
-            for a in range(2):
-                for b in range(2):
-                    if (k, a, b) != (0, 0, 0):
-                        direct_copy(hi, k, a, b).wait_send()
-
-        @pl.when(xh != hi)
-        def _():
-            direct_copy(hi, 0, 0, 0).wait_send()
-            for n in range(last):
-                row_copy(n, hi, 0, 0).wait_send()
+    for n in range(CHUNKS):
+        for hi in range(2):
+            if n < relayed:
+                for k in range(1, rows_z):
+                    z_copy(n, hi, k).wait_send()
+                for a, b in ((1, 0), (1, 1), (0, 1)):
+                    row_copy(n, hi, a, b).wait_send()
+            else:
+                for k in range(rows_z):
+                    for a in range(2):
+                        for b in range(2):
+                            if (k, a, b) != (0, 0, 0):
+                                direct_copy(n, hi, k, a, b).wait_send()
+
+            @pl.when(xh != hi)
+            def _():
+                if n < relayed:
+                    row_copy(n, hi, 0, 0).wait_send()
+                else:
+                    direct_copy(n, hi, 0, 0, 0).wait_send()
 
 
 def in_hbm(array):
@@ -420,8 +430,8 @@
             dma((2 * CHUNKS, rows_z)),
             dma((CHUNKS, 2, 4)),
             dma((CHUNKS, 8)),
-            dma((2, rows_z, 4)),
-            dma,
+            dma((DIRECT, 2, rows_z, 4)),
+            dma((DIRECT,)),
             dma,
             pltpu.SemaphoreType.REGULAR,
             pltpu.SemaphoreType.REGULAR,

time: 60.5 us -> 59.2 us (0.979)
  Pallas kernels: 59.4 us -> 58.1 us
    pallas_call x1, Pallas kernels: 59.4 us -> 58.1 us  [local(): pl.pallas_call(functools.partial(stack_kernel, rows_y, rows_z), name='sta...]
where the time goes in v4:
time: 59.2 us; the launch traced here: 59 us
  Pallas kernels  58.1 us (98%)
  local copies, waits for them, and re-layouts  0.97 us (2%)
    pallas_call x1, Pallas kernels, local(): pl.pallas_call(functools.partial(stack_kernel, rows_y, rows_z), name='sta...  58.1 us

profile of v4, /device:TPU:1, one launch (start us, length us, event | category | flops | bytes accessed | tf_op | source)
XLA Modules:
  0.0 59.0 jit_solution(11302445427728854337)
XLA Ops:
  0.0 58.1 %stack.1 = bf16[2,1,256,1024]{3,2,1,0:T(8,128)(2,1)S(1)} custom-call(bf16[1,32,240,128]{3,2,1,0:T(8,128)(2,1)} %spectra.1, f32[4,128]{1,0:T(4,128)} %bitcast.1), custom_call_target="tpu_custom_call" | custom-call | tf_op jit(solution)/shard_map/stack/pallas_call | solution.py:408
  58.1 1.0 %copy.4 = bf16[2,1,256,1024]{3,2,1,0:T(8,128)(2,1)} copy(bf16[2,1,256,1024]{3,2,1,0:T(8,128)(2,1)S(1)} %stack.1) | data formatting | bytes 2097152

commit v5 on v4

--- a/solution.py
+++ b/solution.py
@@ -270,8 +270,11 @@
     def wait_direct(n):
         pltpu.make_async_copy(landed.at[n], landed.at[n], direct_recv.at[n - relayed]).wait()
 
+    def relays(n, hi):
+        return n < relayed or (n == relayed and n < last and hi == 1)
+
     def send_wave(n, hi):
-        if n < relayed:
+        if relays(n, hi):
             send_z(n, hi)
         else:
             send_direct(n, hi)
@@ -350,16 +353,20 @@
         for p in range(half_way, len(pieces[n + 1])):
             forward(n + 1, p)
         wave(n + 1, 1)
-    for early in range(2, relayed):
+    for early in range(2, last):
         for hi in (1, 0):
-            send_row(early, hi)
+            if relays(early, hi):
+                send_row(early, hi)
     wait_y(last)
     wave(last, 0)
     for n in range(last):
-        if n < relayed:
-            wait_row(n)
-        else:
-            wait_direct(n)
+        for hi in range(2):
+            @pl.when(xh == hi)
+            def _():
+                if relays(n, hi):
+                    wait_row(n)
+                else:
+                    wait_direct(n)
         sort(n)
     lag_product(0, last)
     wait_direct(last)
@@ -373,7 +380,7 @@
             y_copy(n, p).wait_send()
     for n in range(CHUNKS):
         for hi in range(2):
-            if n < relayed:
+            if relays(n, hi):
                 for k in range(1, rows_z):
                     z_copy(n, hi, k).wait_send()
                 for a, b in ((1, 0), (1, 1), (0, 1)):
@@ -387,7 +394,7 @@
 
             @pl.when(xh != hi)
             def _():
-                if n < relayed:
+                if relays(n, hi):
                     row_copy(n, hi, 0, 0).wait_send()
                 else:
                     direct_copy(n, hi, 0, 0, 0).wait_send()

time: 59.2 us -> 59.4 us (level)
  no operation moved by 1% of the time
where the time goes in v5:
time: 59.4 us; the launch traced here: 59.3 us
  Pallas kernels  58.3 us (98%)
  local copies, waits for them, and re-layouts  0.97 us (2%)
    pallas_call x1, Pallas kernels, local(): pl.pallas_call(functools.partial(stack_kernel, rows_y, rows_z), name='sta...  58.3 us

profile of v5, /device:TPU:1, one launch (start us, length us, event | category | flops | bytes accessed | tf_op | source)
XLA Modules:
  0.0 59.3 jit_solution(4624336859013918344)
XLA Ops:
  0.0 58.3 %stack.1 = bf16[2,1,256,1024]{3,2,1,0:T(8,128)(2,1)S(1)} custom-call(bf16[1,32,240,128]{3,2,1,0:T(8,128)(2,1)} %spectra.1, f32[4,128]{1,0:T(4,128)} %bitcast.1), custom_call_target="tpu_custom_call" | custom-call | tf_op jit(solution)/shard_map/stack/pallas_call | solution.py:415
  58.3 1.0 %copy.4 = bf16[2,1,256,1024]{3,2,1,0:T(8,128)(2,1)} copy(bf16[2,1,256,1024]{3,2,1,0:T(8,128)(2,1)S(1)} %stack.1) | data formatting | bytes 2097152
